TPU v7x, 32 devices: a whole 2x2x4 slice. The times are simulated.
32 devices in a mesh: seq: 8 (over z, y), chan: 4 (over x, core).
Axes of the slice: x: 2, y: 2, z: 4, core: 2. Of those that a mesh axis runs over, the one named last changes fastest.
Arguments:
- tokens: bfloat16 [8192, 512], P('seq', 'chan'), may hold values from -6 to 6
- w_in: bfloat16 [512, 3, 512], P(None, None, 'chan'), may hold values from -0.25 to 0.25
- short_filter: float32 [3, 3, 512], P(None, None, 'chan'), may hold values from -3 to 3
- long_filter: float32 [8192, 512], P('seq', 'chan'), may hold values from -0.0625 to 0.0625
- skip_gain: float32 [512], P('chan'), may hold values from 0.5 to 1.5
- w_out: bfloat16 [512, 512], P('chan'), may hold values from -0.25 to 0.25
Outputs:
- mixed: bfloat16 [8192, 512], P('seq', 'chan')
All inputs are finite; a program needn't handle non-finite values.
Results may differ from a plain program's by a relative error of at most 0.007.
Values may be sent and summed in bfloat16 or wider, within the bound.
A program may use at most 64 MiB of HBM per device.

v0:
```python
import functools
import math

import jax
import jax.numpy as jnp
import numpy as np
from jax import lax
from jax.experimental import pallas as pl
from jax.experimental.pallas import tpu as pltpu
from jax.sharding import PartitionSpec as P

MESH = pl.DeviceIdType.MESH
LANES = 128
RIM = 16
F32 = jnp.float32
BF16 = jnp.bfloat16


def split(values):
    high = values.astype(BF16)
    low = (values - high.astype(F32)).astype(BF16)
    return high, low


def split_table(table):
    table = np.asarray(table, np.float64)
    high = table.astype(np.float32).astype(BF16)
    low = (table - high.astype(np.float64)).astype(np.float32).astype(BF16)
    return high, low


def tables(total):
    first = total // LANES
    half = first // 2
    kept = half + 1
    padded = -(-kept // 16) * 16
    k1 = np.arange(padded)
    live = (k1 < kept).astype(np.float64)[:, None]
    n1 = np.arange(half)
    angle = 2.0 * math.pi / first * (k1[:, None] * n1[None, :] % first)
    outer = np.concatenate([np.cos(angle) * live, -np.sin(angle) * live], axis=0)
    outer_table = np.concatenate(split_table(outer), axis=1).astype(np.float32)
    n2 = np.arange(LANES)
    turn = 2.0 * math.pi / total * (k1[:, None] * n2[None, :] % total)
    turn_table = np.stack([np.cos(turn), -np.sin(turn)]).astype(np.float32)
    inner = 2.0 * math.pi / LANES * (n2[:, None] * n2[None, :] % LANES)
    cosine, sine = np.cos(inner), -np.sin(inner)
    ahead = np.block([[cosine, sine], [-sine, cosine]])
    ahead_table = ahead.astype(np.float32)
    back_table = ahead.T.astype(np.float32)
    weight = np.where((k1 == 0) | (k1 == half), 1.0, 2.0) * live[:, 0] / total
    close = np.concatenate([np.cos(angle).T * weight, -np.sin(angle).T * weight], axis=1)
    close_table = close.astype(np.float32)
    return outer_table, turn_table, ahead_table, back_table, close_table


def dot(left, right):
    return jnp.dot(left, right, preferred_element_type=F32)


def each(low, high, body):
    def one(i, carry):
        body(i)
        return carry

    lax.fori_loop(low, high, one, 0)


def piece(start, size):
    return pl.ds(pl.multiple_of(start, size), size)


def dot2(left, table_ref):
    rounded = left.astype(BF16)
    return dot(rounded, table_ref[0]) + dot(rounded, table_ref[1])


def kernel(
    shards, chans, chunks, parts, group, many,
    tok, w_in, sfilt_a, lfilt_a, gain_a, w_out, outer_a, turn_a, ahead_a, back_a, close_a,
    out,
    tbuf, tmini, w, sfilt, lfilt, gain, outer_f, turn_t, ahead_f, back_f, close_f,
    outer_t, ahead_t, back_t, close_t,
    proj, rim_out, rim_in, keep, keep_t, skip_t, stage, h_stage, hs, hr, xs, xr, ys, yr,
    x32, h32, hspec, y32, c32, gbuf, wbuf, w32, w_rows, wt, acc, gain_rows,
    local, tok_send, tok_recv, fwd_send, wo_send, wo_recv, rim_send, rim_recv,
    h_send, h_recv, x_send, x_recv, y_send, y_recv, g_send, g_recv, gf_send,
):
    seq = lax.axis_index("seq")
    chan = lax.axis_index("chan")
    count = tok.shape[0]
    blocks = count // LANES
    cd = LANES // shards
    groups = cd // group
    lots = cd // many
    per = many // group
    rows = count // chunks
    core_peer = chan + 1 - 2 * (chan % 2)
    x_peer = (chan + 2) % chans
    diag = (core_peer + 2) % chans
    others = (core_peer, x_peer, diag)
    far_first = sorted(range(1, shards), key=lambda d: -min(d, shards - d))

    own_columns = pl.ds(pl.multiple_of(chan * LANES, LANES), LANES)
    loads = [(lfilt_a, lfilt), (tok, tbuf.at[chan]), (tok.at[pl.ds(count - RIM, RIM)], tmini.at[chan])]
    loads += [(w_in.at[g], w.at[:, pl.ds(g * LANES, LANES)]) for g in range(3)]
    loads += [(sfilt_a, sfilt), (gain_a, gain), (w_out.at[:, own_columns], wbuf.at[chan])]
    loads += [(outer_a, outer_f), (turn_a, turn_t), (ahead_a, ahead_f), (back_a, back_f), (close_a, close_f)]
    copies = [pltpu.make_async_copy(src, dst, local.at[i]) for i, (src, dst) in enumerate(loads)]
    for copy in copies:
        copy.start()

    barrier = pltpu.get_barrier_semaphore()
    for peer in others:
        pl.semaphore_signal(barrier, inc=1, device_id=(seq, peer), device_id_type=MESH)

    @functools.partial(each, 1, shards)
    def greet(d):
        peer = (seq + d) % shards
        pl.semaphore_signal(barrier, inc=1, device_id=(peer, chan), device_id_type=MESH)

    def spread(turned, block):
        for dest in range(shards):
            stage[dest, piece(block * cd, cd), :] = turned[dest * cd:(dest + 1) * cd, :]

    def pack(dst, part, pieces):
        size = blocks // pieces * cd
        span = piece(part * size, size)
        dst[:, span, :] = stage[:, span, :].astype(BF16)

    copies[0].wait()
    @functools.partial(each, 0, blocks)
    def spread_filter(block):
        turned = lfilt[piece(block * LANES, LANES), :].T
        for dest in range(shards):
            for g in range(lots):
                start = dest * cd + g * many
                h_stage[g, dest, piece(block * many, many), :] = turned[start:start + many, :]

    hs[...] = h_stage[...].astype(BF16)
    for copy in copies[1:]:
        copy.wait()
    gain_rows[...] = jnp.broadcast_to(gain[...], (LANES, LANES)).T
    outer_t[...] = outer_f[...].astype(BF16)
    for table, ref in ((ahead_f, ahead_t), (back_f, back_t), (close_f, close_t)):
        high, low = split(table[...])
        ref[0] = high
        ref[1] = low
    pl.semaphore_wait(barrier, len(others) + shards - 1)

    def remote(src, dst, send, recv, device):
        return pltpu.make_async_remote_copy(
            src_ref=src, dst_ref=dst, send_sem=send, recv_sem=recv,
            device_id=device, device_id_type=MESH,
        )

    def first(k):
        return isinstance(k, int) and k == 0

    def landing(k, owner):
        if first(k):
            return tmini.at[owner]
        return tbuf.at[owner, piece((k - 1) * rows, rows)]

    def tok_copy(k, slot, peer, owner):
        span = pl.ds(count - RIM, RIM) if first(k) else piece((k - 1) * rows, rows)
        return remote(tok.at[span], landing(k, owner), tok_send.at[slot, k], tok_recv.at[owner, k], (seq, peer))

    def fwd_copy(k, owner):
        return remote(landing(k, owner), landing(k, owner), fwd_send.at[k], tok_recv.at[owner, k], (seq, core_peer))

    def give(k):
        tok_copy(k, 1, x_peer, chan).start()
        tok_copy(k, 0, core_peer, chan).start()

    give(0)
    each(1, chunks + 1, give)

    def wo_copy(slot, peer, owner):
        columns = pl.ds(pl.multiple_of(peer * LANES, LANES), LANES)
        return remote(w_out.at[:, columns], wbuf.at[owner], wo_send.at[slot], wo_recv.at[owner], (seq, peer))

    def swap_all(action, src, dst, send, recv, part, span):
        if action == "start":
            for d in far_first:
                peer = (seq + d) % shards
                remote(src.at[peer, span], dst.at[seq, span], send.at[part], recv.at[part], (peer, chan)).start()
            return
        several = pl.ds(0, shards - 1)
        whole = remote(
            src.at[several, span], dst.at[several, span], send.at[part], recv.at[part], ((seq + 1) % shards, chan)
        )
        if action == "recv":
            whole.wait_recv()
        else:
            whole.wait_send()

    def h_swap(action, g):
        swap_all(action, hs.at[g], hr.at[g], h_send, h_recv, g, pl.ds(0, blocks * many))

    def x_swap(action, part):
        size = blocks // parts * cd
        swap_all(action, xs, xr, x_send, x_recv, part, piece(part * size, size))

    def y_swap(action, g):
        swap_all(action, ys.at[g], yr.at[g], y_send, y_recv, g, pl.ds(0, group * blocks))

    h_swap("start", 0)
    for g in range(lots):
        hr[g, seq] = hs[g, seq]
    for slot, peer in enumerate(others):
        wo_copy(slot, peer, chan).start()

    def shorten(k):
        for g in range(3):
            lanes = slice(g * LANES, (g + 1) * LANES)
            base = pl.multiple_of(RIM // 2 + k * rows, 8)
            window = proj[pl.ds(base, rows + 8), lanes]
            value = (
                sfilt[0, g:g + 1, :] * window[8:, :]
                + sfilt[1, g:g + 1, :] * window[7:-1, :]
                + sfilt[2, g:g + 1, :] * window[6:-2, :]
            )
            if g == 0:
                held = value
            elif g == 1:
                held = held * value
            else:
                keep[piece(k * rows, rows), :] = value
        for j in range(rows // LANES):
            block = k * (rows // LANES) + j
            turned = held[j * LANES:(j + 1) * LANES, :].T
            spread(turned, block)
            skip_t[piece(block * LANES, LANES), :] = turned * gain_rows[...]

    def rim_copy():
        return remote(rim_out, rim_in, rim_send, rim_recv, ((seq + 1) % shards, chan))

    def lead(k):
        tok_copy(k, 1, x_peer, x_peer).wait_recv()
        fwd_copy(k, x_peer).start()

    def take(k):
        tok_copy(k, 0, core_peer, core_peer).wait_recv()
        tok_copy(k, 0, core_peer, diag).wait_recv()

    lead(0)
    take(0)
    tail = jnp.concatenate([tmini[j] for j in range(chans)], axis=1)
    rim_out[...] = dot(tail, w[...]).astype(BF16)
    rim_copy().start()
    lead(1)
    @functools.partial(each, 0, parts)
    def project(part):
        for i in range(chunks // parts):
            k = part * (chunks // parts) + i
            pl.when(k + 1 < chunks)(lambda: lead(k + 2))
            take(k + 1)
            span = piece(k * rows, rows)
            features = jnp.concatenate([tbuf[j, span, :] for j in range(chans)], axis=1)
            projected = dot(features, w[...]).astype(BF16)
            proj[pl.ds(pl.multiple_of(RIM + k * rows, RIM), rows), :] = projected.astype(F32)
            if i == 0:
                @pl.when(part == 0)
                def edge_rows():
                    rim_copy().wait_recv()
                    live = (seq > 0).astype(F32)
                    proj[0:RIM, :] = rim_in[...].astype(F32) * live
            shorten(k)
        pack(xs, part, parts)
        x_swap("start", part)
        for j in range(blocks // parts):
            span = piece((part * (blocks // parts) + j) * LANES, LANES)
            keep_t[span, :] = keep[span, :].T

    for g in range(1, lots):
        h_swap("start", g)
    xr[seq] = xs[seq]

    height = shards * blocks
    padded = turn_t.shape[1]
    edge = group * padded

    def spectrum(ref, start, size, stride, product):
        columns = [ref[pl.ds(start + j, height, stride=stride), :].astype(BF16) for j in range(size)]
        signal = jnp.concatenate(columns, axis=1)
        signal = jnp.concatenate([signal, signal], axis=0)
        opened = dot(outer_t[...], signal)
        cosine, sine = turn_t[0], turn_t[1]
        turned = []
        for j in range(size):
            real = opened[:padded, j * LANES:(j + 1) * LANES]
            imag = opened[padded:, j * LANES:(j + 1) * LANES]
            turned.append(jnp.concatenate([real * cosine - imag * sine, real * sine + imag * cosine], axis=1))
        return product(jnp.concatenate(turned, axis=0), ahead_t)

    def dot1(left, table_ref):
        return dot(left.astype(BF16), table_ref[0])

    def filter_spectra(g):
        h_swap("recv", g)
        h32[...] = hr[g].reshape(h32.shape).astype(F32)
        hspec[g] = spectrum(h32, 0, many, many, dot2)

    filter_spectra(0)
    acc[...] = jnp.zeros_like(acc)

    for part in range(parts):
        x_swap("recv", part)
    x32[...] = xr[...].reshape(x32.shape).astype(F32)

    def convolve(g):
        spectra = spectrum(x32, g * group, group, cd, dot1)
        xr_, xi_ = spectra[:, :LANES], spectra[:, LANES:]
        at = piece(g % per * edge, edge)
        hr_, hi_ = hspec[g // per, at, :LANES], hspec[g // per, at, LANES:]
        product = jnp.concatenate([xr_ * hr_ - xi_ * hi_, xr_ * hi_ + xi_ * hr_], axis=1)
        back = dot1(product, back_t)
        cosine, sine = turn_t[0], turn_t[1]
        sums = []
        for j in range(group):
            real = back[j * padded:(j + 1) * padded, :LANES]
            imag = back[j * padded:(j + 1) * padded, LANES:]
            sums.append(jnp.concatenate([real * cosine + imag * sine, imag * cosine - real * sine], axis=0))
        conv = dot(close_t[0], jnp.concatenate(sums, axis=1).astype(BF16))
        for j in range(group):
            y32[:, j * blocks:(j + 1) * blocks, :] = conv[:, j * LANES:(j + 1) * LANES].reshape(shards, blocks, LANES)
        ys[g] = y32[...].astype(BF16)
        y_swap("start", g)
        yr[g, seq] = ys[g, seq]

    def gated_copy(g, slot, peer, owner):
        return remote(gbuf.at[chan, g], gbuf.at[owner, g], g_send.at[slot, g], g_recv.at[owner, g], (seq, peer))

    def gated_fwd(g, owner):
        return remote(gbuf.at[owner, g], gbuf.at[owner, g], gf_send.at[g], g_recv.at[owner, g], (seq, core_peer))

    def gate(g):
        y_swap("recv", g)
        c32[...] = yr[g].reshape(c32.shape).astype(F32)
        for block in range(blocks):
            pieces = []
            for c in range(group):
                conv = c32[pl.ds(c * blocks + block, shards, stride=group * blocks), :]
                at = pl.ds(block * LANES + g * group + c, shards, stride=cd)
                pieces.append(keep_t[at, :] * (conv + skip_t[at, :]))
            gbuf[chan, g, :, block * LANES:(block + 1) * LANES] = jnp.concatenate(pieces, axis=0).astype(BF16)
        gated_copy(g, 1, x_peer, chan).start()
        gated_copy(g, 0, core_peer, chan).start()

    def forward(g):
        gated_copy(g, 1, x_peer, x_peer).wait_recv()
        gated_fwd(g, x_peer).start()

    def mix(g):
        gated_copy(g, 0, core_peer, core_peer).wait_recv()
        gated_copy(g, 0, core_peer, diag).wait_recv()
        whole = jnp.concatenate([gbuf[j, g] for j in range(chans)], axis=0)
        acc[...] += dot(wt[g], whole)

    def meanwhile():
        for slot, peer in enumerate(others):
            wo_copy(slot, peer, peer).wait_recv()

        @functools.partial(each, 0, chans)
        def turn_weights(j):
            w32[...] = wbuf[j].astype(F32)
            for g in range(groups):
                picked = [w32[pl.ds(g * group + c, shards, stride=cd), :] for c in range(group)]
                w_rows[g, j] = jnp.concatenate(picked, axis=0)

        @functools.partial(each, 0, groups)
        def pack_weights(g):
            wt[g] = jnp.concatenate([w_rows[g, j] for j in range(chans)], axis=0).T.astype(BF16)

        def settle(k):
            tok_copy(k, 1, x_peer, chan).wait_send()
            tok_copy(k, 0, core_peer, chan).wait_send()
            fwd_copy(k, x_peer).wait_send()

        settle(0)
        each(1, chunks + 1, settle)
        for slot, peer in enumerate(others):
            wo_copy(slot, peer, chan).wait_send()
        rim_copy().wait_send()
        each(0, lots, lambda g: h_swap("send", g))

    @functools.partial(each, 0, groups + 1)
    def stream(g):
        pl.when((g >= 1) & (g < groups) & (g % per == 0))(lambda: filter_spectra(g // per))
        pl.when(g < groups)(lambda: convolve(g))
        pl.when(g >= 2)(lambda: forward(g - 2))
        pl.when(g >= 1)(lambda: gate(g - 1))
        pl.when(g == groups - 1)(meanwhile)
        pl.when(g >= 3)(lambda: mix(g - 3))

    forward(groups - 1)
    each(0, parts, lambda part: x_swap("send", part))
    each(0, groups, lambda g: y_swap("send", g))
    each(max(groups - 2, 0), groups, mix)
    for block in range(blocks):
        span = slice(block * LANES, (block + 1) * LANES)
        out[span, :] = acc[:, span].T.astype(BF16)

    @functools.partial(each, 0, groups)
    def finish(g):
        gated_copy(g, 1, x_peer, chan).wait_send()
        gated_copy(g, 0, core_peer, chan).wait_send()
        gated_fwd(g, x_peer).wait_send()


def on_device(shards, chans, tokens, w_in, short_filter, long_filter, skip_gain, w_out):
    count, width = tokens.shape
    length = shards * count
    blocks = count // LANES
    cd = width // shards
    chunks = 4
    parts = 4 if blocks // 4 * cd % 16 == 0 else 2
    group = min(cd, 8)
    many = min(cd, 8)
    groups = cd // group
    consts = tables(2 * length)
    outer, turn, ahead, back, close = consts
    wide = 3 * width
    inputs = w_in.shape[0]
    dma = pltpu.SemaphoreType.DMA
    vmem = pltpu.VMEM
    swap_shape = (shards, blocks * cd, LANES)
    flat_shape = (shards * blocks * cd, LANES)
    back_shape = (groups, shards, group * blocks, LANES)
    filter_shape = (cd // many, shards, many * blocks, LANES)
    operands = (
        tokens, w_in.transpose(1, 0, 2), short_filter, long_filter,
        skip_gain.reshape(1, width), w_out,
    ) + tuple(jnp.asarray(c) for c in consts)
    return pl.pallas_call(
        functools.partial(kernel, shards, chans, chunks, parts, group, many),
        out_shape=jax.ShapeDtypeStruct((count, width), BF16),
        in_specs=[pl.BlockSpec(memory_space=pl.ANY)] * len(operands),
        out_specs=pl.BlockSpec(memory_space=vmem),
        scratch_shapes=[
            vmem((chans, count, width), BF16),
            vmem((chans, RIM, width), BF16),
            vmem((inputs, wide), BF16),
            vmem(short_filter.shape, F32),
            vmem((count, width), F32),
            vmem((1, width), F32),
        ] + [vmem(c.shape, F32) for c in consts] + [
            vmem(outer.shape, BF16),
            vmem((2,) + ahead.shape, BF16),
            vmem((2,) + back.shape, BF16),
            vmem((2,) + close.shape, BF16),
            vmem((RIM + count, wide), F32),
            vmem((RIM, wide), BF16),
            vmem((RIM, wide), BF16),
            vmem((count, width), F32),
            vmem((blocks * LANES, LANES), F32),
            vmem((blocks * LANES, LANES), F32),
            vmem(swap_shape, F32),
            vmem(filter_shape, F32),
            vmem(filter_shape, BF16),
            vmem(filter_shape, BF16),
            vmem(swap_shape, BF16),
            vmem(swap_shape, BF16),
            vmem(back_shape, BF16),
            vmem(back_shape, BF16),
            vmem(flat_shape, F32),
            vmem((shards * many * blocks, LANES), F32),
            vmem((cd // many, many * turn.shape[1], 2 * LANES), F32),
            vmem(back_shape[1:], F32),
            vmem((shards * group * blocks, LANES), F32),
            vmem((chans, groups, group * shards, count), BF16),
            vmem((chans, width, LANES), BF16),
            vmem((width, LANES), F32),
            vmem((groups, chans, group * shards, LANES), F32),
            vmem((groups, LANES, chans * group * shards), BF16),
            vmem((LANES, count), F32),
            vmem((LANES, LANES), F32),
            dma((14,)),
            dma((2, chunks + 1)), dma((chans, chunks + 1)), dma((chunks + 1,)),
            dma((3,)), dma((chans,)), dma, dma,
            dma((cd // many,)), dma((cd // many,)),
            dma((parts,)), dma((parts,)),
            dma((groups,)), dma((groups,)),
            dma((2, groups)), dma((chans, groups)), dma((groups,)),
        ],
        compiler_params=pltpu.CompilerParams(
            collective_id=0, has_side_effects=True, vmem_limit_bytes=56 * 1024 * 1024
        ),
        cost_estimate=pl.CostEstimate(flops=4 * 10**9, bytes_accessed=4 * 10**6, transcendentals=0),
    )(*operands)


def solution(mesh):
    shards, chans = mesh.shape["seq"], mesh.shape["chan"]
    return jax.shard_map(
        functools.partial(on_device, shards, chans),
        mesh=mesh,
        in_specs=(
            P("seq", "chan"),
            P(None, None, "chan"),
            P(None, None, "chan"),
            P("seq", "chan"),
            P("chan"),
            P("chan", None),
        ),
        out_specs=P("seq", "chan"),
        check_vma=False,
    )
```

profile of v0, /device:TPU:1, one launch (start us, length us, event | category | flops | bytes accessed | tf_op | source)
XLA Modules:
  0.0 41.1 jit_solution(15404616206760591629)
XLA Ops:
  0.0 39.4 %shard_map.109 = bf16[1024,128]{1,0:T(8,128)(2,1)} custom-call(bf16[1024,128]{1,0:T(8,128)(2,1)} %tok.1, bf16[3,512,128]{2,1,0:T(8,128)(2,1)} %bitcast.2, f32[3,3,128]{2,1,0:T(4,128)} %sfilt_a.1, f32[1024,128]{1,0:T(8,128)} %lfilt_a.1, f32[1,128]{1,0:T(1,128)} %bitcast.3, bf16[128,512]{1,0:T(8,128)(2,1)} %w_out.1, f32[160,128]{1,0:T(8,128)} %constant.10.clone.outer_a, ...), custom_call_target="tpu_custom_call" | custom-call | flops 4000000000 | bytes 4000000 | tf_op jit(solution)/shard_map/pallas_call | solution.py:436
  39.4 1.7 %copy.13 = bf16[1024,128]{1,0:T(8,128)(2,1)} copy(bf16[1024,128]{1,0:T(8,128)(2,1)} %shard_map.109) | data formatting | bytes 524288
where the time goes:
time: 41.3 us; the launch traced here: 41.1 us
  Pallas kernels  39.4 us (95%)
  local copies, waits for them, and re-layouts  1.67 us (4%)
    pallas_call x1, Pallas kernels, on_device(): pl.pallas_call(functools.partial(kernel, shards, chans, chunks, parts, gr...  39.4 us
    unnamed x1, local copies, waits for them, and re-layouts  1.67 us

commit v1 on v0

--- a/solution.py
+++ b/solution.py
@@ -414,8 +414,8 @@
     length = shards * count
     blocks = count // LANES
     cd = width // shards
-    chunks = 4
-    parts = 4 if blocks // 4 * cd % 16 == 0 else 2
+    chunks = 2
+    parts = 2
     group = min(cd, 8)
     many = min(cd, 8)
     groups = cd // group

time: 41.3 us -> 43.2 us (1.046)
  Pallas kernels: 39.4 us -> 41.4 us
    pallas_call x1, Pallas kernels: 39.4 us -> 41.4 us  [on_device(): pl.pallas_call(functools.partial(kernel, shards, chans, chunks, parts, gr...]
where the time goes in v1:
time: 43.2 us; the launch traced here: 43 us
  Pallas kernels  41.4 us (96%)
  local copies, waits for them, and re-layouts  1.67 us (4%)
    pallas_call x1, Pallas kernels, on_device(): pl.pallas_call(functools.partial(kernel, shards, chans, chunks, parts, gr...  41.4 us
    unnamed x1, local copies, waits for them, and re-layouts  1.67 us

profile of v1, /device:TPU:1, one launch (start us, length us, event | category | flops | bytes accessed | tf_op | source)
XLA Modules:
  0.0 43.0 jit_solution(8336695003444134390)
XLA Ops:
  0.0 41.4 %shard_map.109 = bf16[1024,128]{1,0:T(8,128)(2,1)} custom-call(bf16[1024,128]{1,0:T(8,128)(2,1)} %tok.1, bf16[3,512,128]{2,1,0:T(8,128)(2,1)} %bitcast.2, f32[3,3,128]{2,1,0:T(4,128)} %sfilt_a.1, f32[1024,128]{1,0:T(8,128)} %lfilt_a.1, f32[1,128]{1,0:T(1,128)} %bitcast.3, bf16[128,512]{1,0:T(8,128)(2,1)} %w_out.1, f32[160,128]{1,0:T(8,128)} %constant.10.clone.outer_a, ...), custom_call_target="tpu_custom_call" | custom-call | flops 4000000000 | bytes 4000000 | tf_op jit(solution)/shard_map/pallas_call | solution.py:436
  41.4 1.7 %copy.13 = bf16[1024,128]{1,0:T(8,128)(2,1)} copy(bf16[1024,128]{1,0:T(8,128)(2,1)} %shard_map.109) | data formatting | bytes 524288
